TPU v7x, 32 devices: a whole 2x2x4 slice. The times are simulated.
32 devices in a mesh: groups: 2 (over x), epoch: 4 (over y, core), space: 4 (over z).
Axes of the slice: x: 2, y: 2, z: 4, core: 2. Of those that a mesh axis runs over, the one named last changes fastest.
Arguments:
- slc_stack: bfloat16 [2, 32, 32, 960], P(None, ('epoch', 'space'), 'groups'), parts along dimension 2, may hold values from -45 to 45
Outputs:
- coherence: bfloat16 [2, 32, 32, 2048], P(None, 'epoch', None, ('groups', 'space')), parts along dimension 3
There are 2 independent parts, one for each index of `groups`. A program takes and returns all parts, laid end to end along the dimension named above; each array names one. Nothing has to cross between parts.
All inputs are finite; a program needn't handle non-finite values.
Results may differ from a plain program's by a relative error of at most 0.001.
Values may be sent and summed in bfloat16 or wider, within the bound.
A program may use at most 128 MiB of HBM per device.

v0:
```python
import jax
import jax.numpy as jnp
from jax import lax
from jax.sharding import PartitionSpec as P

LOOKR = 5
LOOKC = 15
MARGIN = 2


def extended(cells, sides, width):
    for axis, dim in sides:
        count = lax.axis_size(axis)
        ends = count - 1
        head = lax.slice_in_dim(cells, 0, width, axis=dim)
        tail = lax.slice_in_dim(cells, cells.shape[dim] - width, cells.shape[dim], axis=dim)
        cells = jnp.concatenate(
            [
                lax.ppermute(tail, axis, [(i, (i + 1) % count) for i in range(ends)]),
                cells,
                lax.ppermute(head, axis, [((i + 1) % count, i) for i in range(ends)]),
            ],
            axis=dim,
        )
    return cells


def window_sums(values_in):
    row_count = values_in.shape[-2] - 2 * MARGIN
    col_count = values_in.shape[-1] // LOOKC
    folded = values_in.reshape(values_in.shape[:-1] + (col_count, LOOKC)).sum(-1)
    running = folded[..., 0:row_count, :]
    for offset in range(1, LOOKR):
        running = running + folded[..., offset : offset + row_count, :]
    return running


def powers_of(strip_data):
    real_part = strip_data[0].astype(jnp.float32)
    imag_part = strip_data[1].astype(jnp.float32)
    return window_sums(real_part * real_part + imag_part * imag_part) + 1e-06


def pair_coherence(left_strip, right_strip, left_power, right_power):
    left_re = left_strip[0].astype(jnp.float32)[:, None]
    left_im = left_strip[1].astype(jnp.float32)[:, None]
    right_re = right_strip[0].astype(jnp.float32)[None]
    right_im = right_strip[1].astype(jnp.float32)[None]
    cross_re = window_sums(left_re * right_re + left_im * right_im)
    cross_im = window_sums(left_im * right_re - left_re * right_im)
    inverse = lax.rsqrt(left_power[:, None] * right_power[None])
    return jnp.stack([cross_re * inverse, cross_im * inverse]).astype(jnp.bfloat16)


def per_device(slc_stack):
    local_epochs = slc_stack.shape[1]
    all_rows = slc_stack.shape[2]
    col_total = slc_stack.shape[3]
    space_count = lax.axis_size("space")
    epoch_count = lax.axis_size("epoch")
    strip_rows = all_rows // space_count
    block_epochs = local_epochs * space_count
    look_cols = col_total // LOOKC
    cores = slc_stack.reshape(2, local_epochs, space_count, strip_rows, col_total)
    held_rows = cores.shape[3]
    col_width = col_total // epoch_count
    parted = cores.reshape(2, 1, 1, local_epochs, space_count, held_rows, epoch_count, col_width)
    moved = lax.all_to_all(
        lax.all_to_all(parted, "epoch", split_axis=6, concat_axis=1, tiled=True),
        "space",
        split_axis=4,
        concat_axis=2,
        tiled=True,
    )
    held = moved.reshape(2, local_epochs * space_count * epoch_count, held_rows, col_width)
    held = extended(held, (("space", 2),), MARGIN)
    own_power = powers_of(held)
    epochs_all = held.shape[1]

    def one_block(block_index):
        first = block_index * block_epochs
        left_strip = lax.dynamic_slice_in_dim(held, first, block_epochs, 1)
        left_power = lax.dynamic_slice_in_dim(own_power, first, block_epochs, 0)
        return pair_coherence(left_strip, held, left_power, own_power)

    blocks = lax.map(one_block, jnp.arange(epoch_count, dtype=jnp.int32))
    joined = jnp.transpose(blocks, (1, 0, 2, 3, 4, 5)).reshape(
        2, epochs_all, epochs_all, strip_rows, own_power.shape[-1]
    )
    returned_all = lax.all_to_all(joined, "epoch", split_axis=1, concat_axis=4, tiled=True)
    return returned_all.reshape(2, block_epochs, epochs_all, strip_rows * look_cols)


def solution(mesh):
    in_specs = (P(None, ("epoch", "space"), "groups", None),)
    out_specs = P(None, "epoch", None, ("groups", "space"))
    return jax.shard_map(
        per_device, mesh=mesh, in_specs=in_specs, out_specs=out_specs, check_vma=False
    )
```

profile of v0, /device:TPU:0, one launch (start us, length us, event | category | flops | bytes accessed | tf_op | source)
XLA Modules:
  0.0 79.8 jit_solution(2709004483586370430)
XLA Ops:
  0.0 1.1 %reshape_reshape.3 = bf16[2,1,1,2,4,4,4,240]{7,6,5,4,3,0,2,1:T(4,128)(2,1)S(1)} reshape(bf16[2,2,16,960]{3,2,1,0:T(8,128)(2,1)} %param.3) | data formatting | bytes 245760 | tf_op jit(solution)/shard_map/reshape;reshape | solution.py:67
  1.1 8.7 %all_to_all.48 = bf16[2,1,1,2,4,4,4,240]{7,5,3,4,0,2,1,6:T(4,128)(2,1)S(1)} all-to-all(bf16[2,1,1,2,4,4,4,240]{7,5,3,4,0,2,1,6:T(4,128)(2,1)S(1)} %copy.97), channel_id=1, replica_groups=mesh['groups'=2,'epoch'=4,'space'=4] {'epoch'}, dimensions={6} | all-to-all | bytes 245760 | tf_op jit(solution)/shard_map/all_to_all | solution.py:69
  9.9 10.6 %all_to_all.49 = bf16[2,4,1,2,4,4,1,240]{7,5,3,1,0,6,2,4:T(4,128)(2,1)S(1)} all-to-all(bf16[2,4,1,2,4,4,1,240]{7,5,3,1,0,6,2,4:T(4,128)(2,1)S(1)} %copy.98), channel_id=1, replica_groups=mesh['groups'=2,'epoch'=4,'space'=4] {'space'}, dimensions={4} | all-to-all | bytes 245760 | tf_op jit(solution)/shard_map/all_to_all | solution.py:68
  20.6 3.2 %collective-permute-start = (bf16[2,32,2,240]{3,2,1,0:T(2,128)(2,1)S(1)}, bf16[2,32,2,240]{3,2,1,0:T(2,128)(2,1)S(1)}, u32[]{:S(2)}, u32[]{:S(2)}) collective-permute-start(bf16[2,32,2,240]{3,2,1,0:T(2,128)(2,1)S(1)} %get-tuple-element.81), channel_id=1, source_target_pairs={{0,1},{1,2},{2,3},{4,5},{5,6},{6,7},{8,9},{9,10},{10,11},{12,13},{... | collective-permute-start | bytes 184328 | tf_op jit(solution)/shard_map/ppermute | solution.py:19
  23.8 1.3 %collective-permute-start.1 = (bf16[2,32,2,240]{3,2,1,0:T(2,128)(2,1)S(1)}, bf16[2,32,2,240]{3,2,1,0:T(2,128)(2,1)S(1)}, u32[]{:S(2)}, u32[]{:S(2)}) collective-permute-start(bf16[2,32,2,240]{3,2,1,0:T(2,128)(2,1)S(1)} %get-tuple-element.82), channel_id=1, source_target_pairs={{1,0},{2,1},{3,2},{5,4},{6,5},{7,6},{9,8},{10,9},{11,10},{13,12},{... | collective-permute-start | bytes 184328 | tf_op jit(solution)/shard_map/ppermute | solution.py:21
  25.1 0.6 collective-permute-done
  25.7 4.3 %collective-permute-done.1 = bf16[2,32,2,240]{3,2,1,0:T(2,128)(2,1)S(1)} collective-permute-done((bf16[2,32,2,240]{3,2,1,0:T(2,128)(2,1)S(1)}, bf16[2,32,2,240]{3,2,1,0:T(2,128)(2,1)S(1)}, u32[]{:S(2)}, u32[]{:S(2)}) %collective-permute-start.1) | collective-permute-done | bytes 61472 | tf_op jit(solution)/shard_map/ppermute | solution.py:21
  30.8 37.6 %while.10 = (s32[]{:T(128)}, bf16[4,2,8,32,4,16]{3,5,4,2,0,1:T(8,128)(2,1)S(1)}, s32[4]{0:T(128)S(1)}, bf16[2,32,8,240]{3,2,1,0:T(8,128)(2,1)S(1)}, f32[32,4,16]...) while((s32[]{:T(128)}, bf16[4,2,8,32,4,16]{3,5,4,2,0,1:T(8,128)(2,1)S(1)}, ...), condition=%wide.region_4.5_spmd, body=%wide.region_1.4_spmd.sunk | while | flops 4241415 | bytes 4536507 | solution.py:86
  30.8 0.7 dynamic_slice.14
  33.8 0.6 copy.119
  34.6 5.2 %add_reduce_fusion.2 = (f32[8,32,8,16]{1,3,2,0:T(8,128)S(1)}, f32[8,32,8,16]{1,3,2,0:T(8,128)S(1)}) fusion(f32[32,8,16,15]{0,2,3,1:T(8,128)S(1)} %copy.120, f32[8,8,16,15]{2,3,1,0:T(8,128)S(1)} %copy.121, f32[32,8,16,15]{0,2,3,1:T(8,128)S(1)} %copy.122, f32[8,8,16,15]{2,3,1,0:T(8,128)S(1)} %copy.123), kind=kLoop, calls=%fused_computation.1.clone.1 | loop fusion | flops 3866624 | bytes 876544 | tf_op jit(solution)/shard_map/while/body/eval_jaxpr/reduce_sum | solution.py:31
  40.2 0.7 dynamic_slice.14
  43.2 0.6 copy.119
  44.0 5.2 %add_reduce_fusion.2 = (f32[8,32,8,16]{1,3,2,0:T(8,128)S(1)}, f32[8,32,8,16]{1,3,2,0:T(8,128)S(1)}) fusion(f32[32,8,16,15]{0,2,3,1:T(8,128)S(1)} %copy.120, f32[8,8,16,15]{2,3,1,0:T(8,128)S(1)} %copy.121, f32[32,8,16,15]{0,2,3,1:T(8,128)S(1)} %copy.122, f32[8,8,16,15]{2,3,1,0:T(8,128)S(1)} %copy.123), kind=kLoop, calls=%fused_computation.1.clone.1 | loop fusion | flops 3866624 | bytes 876544 | tf_op jit(solution)/shard_map/while/body/eval_jaxpr/reduce_sum | solution.py:31
  49.6 0.7 dynamic_slice.14
  52.6 0.6 copy.119
  53.4 5.2 %add_reduce_fusion.2 = (f32[8,32,8,16]{1,3,2,0:T(8,128)S(1)}, f32[8,32,8,16]{1,3,2,0:T(8,128)S(1)}) fusion(f32[32,8,16,15]{0,2,3,1:T(8,128)S(1)} %copy.120, f32[8,8,16,15]{2,3,1,0:T(8,128)S(1)} %copy.121, f32[32,8,16,15]{0,2,3,1:T(8,128)S(1)} %copy.122, f32[8,8,16,15]{2,3,1,0:T(8,128)S(1)} %copy.123), kind=kLoop, calls=%fused_computation.1.clone.1 | loop fusion | flops 3866624 | bytes 876544 | tf_op jit(solution)/shard_map/while/body/eval_jaxpr/reduce_sum | solution.py:31
  59.0 0.7 dynamic_slice.14
  62.0 0.6 copy.119
  62.8 5.2 %add_reduce_fusion.2 = (f32[8,32,8,16]{1,3,2,0:T(8,128)S(1)}, f32[8,32,8,16]{1,3,2,0:T(8,128)S(1)}) fusion(f32[32,8,16,15]{0,2,3,1:T(8,128)S(1)} %copy.120, f32[8,8,16,15]{2,3,1,0:T(8,128)S(1)} %copy.121, f32[32,8,16,15]{0,2,3,1:T(8,128)S(1)} %copy.122, f32[8,8,16,15]{2,3,1,0:T(8,128)S(1)} %copy.123), kind=kLoop, calls=%fused_computation.1.clone.1 | loop fusion | flops 3866624 | bytes 876544 | tf_op jit(solution)/shard_map/while/body/eval_jaxpr/reduce_sum | solution.py:31
  68.6 1.0 %reshape.97 = bf16[4,2,16384]{2,1,0:T(2,128)(2,1)S(1)} reshape(bf16[32,2,4,16,32]{4,3,2,1,0:T(8,128)(2,1)S(1)} %bitcast.52) | data formatting | bytes 524288
  69.6 8.4 %all_to_all.50 = bf16[4,2,16384]{2,1,0:T(2,128)(2,1)S(1)} all-to-all(bf16[4,2,16384]{2,1,0:T(2,128)(2,1)S(1)} %reshape.97), channel_id=1, replica_groups=mesh['groups'=2,'epoch'=4,'space'=4] {'epoch'}, dimensions={0} | all-to-all | bytes 524288 | tf_op jit(solution)/shard_map/all_to_all | solution.py:90
  78.0 0.5 reshape.98
  78.8 1.0 %copy.106 = bf16[2,8,32,256]{3,2,1,0:T(8,128)(2,1)} copy(bf16[2,8,32,256]{2,3,1,0:T(8,128)(2,1)S(1)} %bitcast.54) | data formatting | bytes 524288 | tf_op jit(solution)/shard_map/reshape | solution.py:91
  (62 shorter events, 10.3 us)
Async XLA Ops:
  20.6 5.1 %collective-permute-start = (bf16[2,32,2,240]{3,2,1,0:T(2,128)(2,1)S(1)}, bf16[2,32,2,240]{3,2,1,0:T(2,128)(2,1)S(1)}, u32[]{:S(2)}, u32[]{:S(2)}) collective-permute-start(bf16[2,32,2,240]{3,2,1,0:T(2,128)(2,1)S(1)} %get-tuple-element.81), channel_id=1, source_target_pairs={{0,1},{1,2},{2,3},{4,5},{5,6},{6,7},{8,9},{9,10},{10,11},{12,13},{... | collective-permute-start | bytes 184328 | tf_op jit(solution)/shard_map/ppermute | solution.py:19
  23.8 6.2 %collective-permute-start.1 = (bf16[2,32,2,240]{3,2,1,0:T(2,128)(2,1)S(1)}, bf16[2,32,2,240]{3,2,1,0:T(2,128)(2,1)S(1)}, u32[]{:S(2)}, u32[]{:S(2)}) collective-permute-start(bf16[2,32,2,240]{3,2,1,0:T(2,128)(2,1)S(1)} %get-tuple-element.82), channel_id=1, source_target_pairs={{1,0},{2,1},{3,2},{5,4},{6,5},{7,6},{9,8},{10,9},{11,10},{13,12},{... | collective-permute-start | bytes 184328 | tf_op jit(solution)/shard_map/ppermute | solution.py:21
where the time goes:
time: 80.2 us; the launch traced here: 79.8 us
  blocking collectives  27.7 us (35%)
  other arithmetic  22.2 us (28%)
  local copies, waits for them, and re-layouts  17.3 us (22%)
  waiting for transfers between devices  4.85 us (6%)
  starting transfers between devices  4.47 us (6%)
  loops' own time  3.18 us (4%)
    reduce_sum x5, other arithmetic, window_sums(): values_in.reshape(values_in.shape[:-1] + (col_count, LOOKC)).sum(-1)  20.8 us
    all_to_all x1, blocking collectives, per_device(): lax.all_to_all(lax.all_to_all(parted, 'epoch', split_axis=6, concat_axis=...  10.6 us
    all_to_all x1, blocking collectives, per_device(): lax.all_to_all(parted, 'epoch', split_axis=6, concat_axis=1, tiled=True)  8.67 us
    all_to_all x1, blocking collectives, per_device(): lax.all_to_all(joined, 'epoch', split_axis=1, concat_axis=4, tiled=True)  8.42 us
    ppermute x1, waiting for transfers between devices, extended(): lax.ppermute(head, axis, [((i + 1) % count, i) for i in range(ends)])  4.27 us
    another operation x1, loops' own time, per_device(): blocks = lax.map(one_block, jnp.arange(epoch_count, dtype=jnp.int32))  3.18 us
    ppermute x1, starting transfers between devices, extended(): lax.ppermute(tail, axis, [(i, (i + 1) % count) for i in range(ends)])  3.17 us
    convert_element_type x8, local copies, waits for them, and re-layouts, pair_coherence(): left_re = left_strip[0].astype(jnp.float32)[:, None]  3.11 us
  transfers between devices with their start and end apart: 2, of which 2 were waited for; matrix products, arithmetic and copies ran while one was open for 0% of the time, Pallas kernels for 0%

commit v1 on v0

v1 whole, which is shorter than its diff:
```python
import functools

import jax
import jax.numpy as jnp
from jax import lax
from jax.experimental import pallas as pl
from jax.experimental.pallas import tpu as pltpu
from jax.sharding import PartitionSpec as P

LOOKR = 5
LOOKC = 15
MARGIN = 2
LANES = 128
MESH = pl.DeviceIdType.MESH
F32 = jnp.float32
BF16 = jnp.bfloat16


def iota(shape, axis):
    return lax.broadcasted_iota(jnp.int32, shape, axis)


def one_hot(hits):
    return jnp.where(hits, 1.0, 0.0).astype(BF16)


def kernel(dims, x_ref, out_ref, strips, parts, epochs, lefts, powers, coh, got, *sems):
    n_epoch, n_space, local, rows, cols, strip = dims
    send1, recv1, send2, recv2 = sems
    total = n_epoch * n_space * local
    block = n_space * local
    held = strip + 2 * MARGIN
    width = cols // n_epoch
    lane_pad = strips.shape[-1] // 2
    looks = width // LOOKC
    all_looks = cols // LOOKC
    lanes = block * looks
    my_i = lax.axis_index("epoch")
    my_j = lax.axis_index("space")
    me = my_i * n_space + my_j

    def epoch_peer(step):
        core = lax.rem(lax.rem(my_i, 2) + step % 2, 2)
        return lax.rem(my_i // 2 + step // 2, n_epoch // 2) * 2 + core

    def epoch_source(step):
        core = lax.rem(lax.rem(my_i, 2) + step % 2, 2)
        return lax.rem(my_i // 2 + n_epoch // 2 - step // 2, n_epoch // 2) * 2 + core

    steps = [
        (a, b)
        for b in reversed(range(n_space))
        for a in reversed(range(n_epoch))
        if a or b
    ]

    barrier = pltpu.get_barrier_semaphore()
    for a, b in steps:
        pl.semaphore_signal(
            barrier,
            inc=1,
            device_id={"epoch": epoch_peer(a), "space": lax.rem(my_j + b, n_space)},
            device_id_type=MESH,
        )

    cut = (n_space * held * local, local * rows)
    at = iota(cut, 0)
    strip_of, row_of, own_of = at // (held * local), (at // local) % held, at % local
    pick_own, pick_row = iota(cut, 1) // rows, iota(cut, 1) % rows
    pick = one_hot((pick_own == own_of) & (pick_row == strip_of * strip + row_of - MARGIN))
    for k in range(2):
        picked = jnp.dot(pick, x_ref[k].reshape(local * rows, cols), preferred_element_type=F32)
        for i in range(n_epoch):
            piece = picked[:, i * width : (i + 1) * width]
            if lane_pad > width:
                piece = jnp.concatenate(
                    [piece, jnp.zeros((piece.shape[0], lane_pad - width), F32)], axis=1
                )
            piece = piece.astype(BF16)
            for j in range(n_space):
                strips[i * n_space + j, :, k * lane_pad : (k + 1) * lane_pad] = piece[
                    j * held * local : (j + 1) * held * local
                ]

    pl.semaphore_wait(barrier, len(steps))

    def first_copy(slot, to_i, to_j, source):
        return pltpu.make_async_remote_copy(
            src_ref=strips.at[to_i * n_space + to_j],
            dst_ref=parts.at[source],
            send_sem=send1.at[slot],
            recv_sem=recv1.at[source],
            device_id={"epoch": to_i, "space": to_j},
            device_id_type=MESH,
        )

    sent = []
    for slot, (a, b) in enumerate(steps):
        copy = first_copy(slot, epoch_peer(a), lax.rem(my_j + b, n_space), me)
        copy.start()
        sent.append(copy)
    parts[me] = strips[me]
    for slot, (a, b) in enumerate(steps):
        from_i, from_j = epoch_source(a), lax.rem(my_j + n_space - b, n_space)
        first_copy(slot, from_i, from_j, from_i * n_space + from_j).wait_recv()

    size = total * held
    to, fro = iota((size, size), 0), iota((size, size), 1)
    order = one_hot(
        (to // total == (fro // local) % held)
        & (to % total == fro // (held * local) * local + fro % local)
    )
    arrived = parts[...]
    if (held * local) % 16:
        arrived = arrived.astype(F32).reshape(size, 2 * lane_pad).astype(BF16)
    else:
        arrived = arrived.reshape(size, 2 * lane_pad)
    by_row = jnp.dot(order, arrived, preferred_element_type=F32)
    epochs[...] = by_row
    re, im = by_row[:, :lane_pad], by_row[:, lane_pad:]
    turned = jnp.concatenate([-im, re], axis=1).astype(BF16)
    plain = by_row.astype(BF16)
    for row in range(held):
        lefts[row, :total] = plain[row * total : (row + 1) * total]
        lefts[row, total:] = turned[row * total : (row + 1) * total]

    square = (re * re + im * im).reshape(held, total, lane_pad)
    summed = [
        functools.reduce(lambda p, q: p + q, [square[r + d] for d in range(LOOKR)])
        for r in range(strip)
    ]
    summed = jnp.concatenate(summed, axis=0)
    look = iota((lane_pad, lanes), 1) % looks
    col = iota((lane_pad, lanes), 0)
    fold = jnp.where((col >= look * LOOKC) & (col < look * LOOKC + LOOKC), 1.0, 0.0)
    power = jnp.dot(summed, fold, preferred_element_type=F32, precision=lax.Precision.HIGHEST)
    power = power + 1e-06
    for r in range(strip):
        powers[r] = power[r * total : (r + 1) * total]

    window = iota((1, looks, 2 * lane_pad), 1) * LOOKC
    place = iota((1, looks, 2 * lane_pad), 2) % lane_pad
    inside = (place >= window) & (place < window + LOOKC)
    own_lane = iota((block, lanes), 1) // looks == iota((block, lanes), 0)

    def second_copy(slot, to_i, source):
        return pltpu.make_async_remote_copy(
            src_ref=coh.at[slot],
            dst_ref=got.at[source],
            send_sem=send2.at[slot],
            recv_sem=recv2.at[source],
            device_id={"epoch": to_i},
            device_id_type=MESH,
        )

    for step in reversed(range(n_epoch)):
        to_i = epoch_peer(step)
        first = to_i * block
        grams = []
        for row in range(held):
            start = row * total + first
            if block % 8 == 0:
                start = pl.multiple_of(start, 8)
            mine = epochs[pl.ds(start, block), :]
            masked = jnp.where(inside, mine[:, None, :], 0.0).astype(BF16)
            grams.append(
                lax.dot_general(
                    lefts[row],
                    masked.reshape(lanes, 2 * lane_pad),
                    (((1,), (1,)), ((), ())),
                    preferred_element_type=F32,
                )
            )
        for r in range(strip):
            cross = functools.reduce(lambda p, q: p + q, grams[r : r + LOOKR])
            left = powers[r, pl.ds(pl.multiple_of(first, 8) if block % 8 == 0 else first, block), :]
            left = jnp.sum(jnp.where(own_lane, left, 0.0), axis=0, keepdims=True)
            inverse = lax.rsqrt(left * powers[r])
            value = jnp.concatenate(
                [cross[:total] * inverse, cross[total:] * inverse], axis=0
            ).astype(BF16)
            if step:
                coh[step, r] = value
            else:
                got[my_i, r] = value
        if step:
            copy = second_copy(step, to_i, my_i)
            copy.start()
            sent.append(copy)

    for step in reversed(range(1, n_epoch)):
        from_i = epoch_source(step)
        second_copy(step, from_i, from_i).wait_recv()

    if lanes == LANES and (strip * n_epoch) % block == 0 and block & (block - 1) == 0:
        spot = iota((2 * total, lanes), 1) // looks
        for half in range(strip * n_epoch // block):
            tiles = []
            for t in range(half * block, (half + 1) * block):
                tiles.append(got[t % n_epoch, t // n_epoch].astype(F32))
            bit = 1
            while bit < block:
                low = (spot // bit) % 2 == 0
                turned_tiles = list(tiles)
                for t in range(block):
                    if t & bit:
                        continue
                    one, two = tiles[t], tiles[t + bit]
                    turned_tiles[t] = jnp.where(low, one, pltpu.roll(two, bit * looks, 1))
                    turned_tiles[t + bit] = jnp.where(
                        low, pltpu.roll(one, lanes - bit * looks, 1), two
                    )
                tiles = turned_tiles
                bit *= 2
            for e in range(block):
                value = tiles[e].astype(BF16)
                for k in range(2):
                    out_ref[k, e, :, half * lanes : (half + 1) * lanes] = value[
                        k * total : (k + 1) * total
                    ]
    else:
        shape = (lanes, strip * all_looks)
        fro_e, fro_c, goal = iota(shape, 0) // looks, iota(shape, 0) % looks, iota(shape, 1)
        for e in range(block):

            def add(i, acc):
                for r in range(strip):
                    spread = one_hot((fro_e == e) & (goal == r * all_looks + i * looks + fro_c))
                    acc = acc + jnp.dot(got[i, r], spread, preferred_element_type=F32)
                return acc

            value = lax.fori_loop(0, n_epoch, add, jnp.zeros((2 * total, shape[1]), F32))
            value = value.astype(BF16)
            for k in range(2):
                out_ref[k, e] = value[k * total : (k + 1) * total]

    for copy in sent:
        copy.wait_send()


def per_device(slc_stack):
    n_epoch, n_space = lax.axis_size("epoch"), lax.axis_size("space")
    _, local, rows, cols = slc_stack.shape
    strip = rows // n_space
    held = strip + 2 * MARGIN
    total = n_epoch * n_space * local
    block = n_space * local
    width = cols // n_epoch
    lane_pad = -(-width // LANES) * LANES
    lanes = block * (width // LOOKC)
    sources = n_epoch * n_space
    dims = (n_epoch, n_space, local, rows, cols, strip)
    vmem = pl.BlockSpec(memory_space=pltpu.VMEM)
    return pl.pallas_call(
        functools.partial(kernel, dims),
        out_shape=jax.ShapeDtypeStruct((2, block, total, strip * (cols // LOOKC)), BF16),
        in_specs=[vmem],
        out_specs=vmem,
        scratch_shapes=[
            pltpu.VMEM((sources, held * local, 2 * lane_pad), BF16),
            pltpu.VMEM((sources, held * local, 2 * lane_pad), BF16),
            pltpu.VMEM((held * total, 2 * lane_pad), F32),
            pltpu.VMEM((held, 2 * total, 2 * lane_pad), BF16),
            pltpu.VMEM((strip, total, lanes), F32),
            pltpu.VMEM((n_epoch, strip, 2 * total, lanes), BF16),
            pltpu.VMEM((n_epoch, strip, 2 * total, lanes), BF16),
            pltpu.SemaphoreType.DMA((sources - 1,)),
            pltpu.SemaphoreType.DMA((sources,)),
            pltpu.SemaphoreType.DMA((n_epoch,)),
            pltpu.SemaphoreType.DMA((n_epoch,)),
        ],
        compiler_params=pltpu.CompilerParams(
            collective_id=0, has_side_effects=True, vmem_limit_bytes=48 * 1024 * 1024
        ),
        cost_estimate=pl.CostEstimate(flops=10**9, bytes_accessed=10**6, transcendentals=0),
    )(slc_stack)


def solution(mesh):
    in_specs = (P(None, ("epoch", "space"), "groups", None),)
    out_specs = P(None, "epoch", None, ("groups", "space"))
    return jax.shard_map(
        per_device, mesh=mesh, in_specs=in_specs, out_specs=out_specs, check_vma=False
    )
```

time: 80.2 us -> 20.9 us (0.26)
  blocking collectives: 27.7 us -> 0 us
  other arithmetic: 22.2 us -> 0 us
  Pallas kernels: 0 us -> 19.1 us
  local copies, waits for them, and re-layouts: 17.3 us -> 1.61 us
  waiting for transfers between devices: 4.85 us -> 0 us
  starting transfers between devices: 4.47 us -> 0 us
  loops' own time: 3.18 us -> 0 us
    all_to_all x3 -> x0, blocking collectives: 27.7 us -> none  [the longest x1 10.6 us: per_device(): lax.all_to_all(lax.all_to_all(parted, 'epoch', split_axis=6, concat_axis=...]
    reduce_sum x5 -> x0, other arithmetic: 20.8 us -> none  [window_sums(): values_in.reshape(values_in.shape[:-1] + (col_count, LOOKC)).sum(-1)]
    pallas_call x0 -> x1, Pallas kernels: none -> 19.1 us  [per_device(): pl.pallas_call(functools.partial(kernel, dims), out_shape=jax.ShapeDtypeS...]
    convert_element_type x16 -> x0, local copies, waits for them, and re-layouts: 6.17 us -> none  [the longest x8 3.11 us: pair_coherence(): left_re = left_strip[0].astype(jnp.float32)[:, None]]
    ppermute x2 -> x0, waiting for transfers between devices: 4.85 us -> none  [the longest x1 4.27 us: extended(): lax.ppermute(head, axis, [((i + 1) % count, i) for i in range(ends)])]
    ppermute x2 -> x0, starting transfers between devices: 4.47 us -> none  [the longest x1 3.17 us: extended(): lax.ppermute(tail, axis, [(i, (i + 1) % count) for i in range(ends)])]
    another operation x6 -> x0, local copies, waits for them, and re-layouts: 3.43 us -> none
    dynamic_slice x12 -> x0, local copies, waits for them, and re-layouts: 3.29 us -> none  [the longest x4 2.67 us: per_device(): blocks = lax.map(one_block, jnp.arange(epoch_count, dtype=jnp.int32))]
  transfers between devices with their start and end apart: 2 -> 0, of which waited for: 2 -> 0; matrix products, arithmetic and copies ran while one was open for 0% -> 0% of each run, Pallas kernels for 0% -> 0%
where the time goes in v1:
time: 20.9 us; the launch traced here: 20.8 us
  Pallas kernels  19.1 us (91%)
  local copies, waits for them, and re-layouts  1.61 us (8%)
    pallas_call x1, Pallas kernels, per_device(): pl.pallas_call(functools.partial(kernel, dims), out_shape=jax.ShapeDtypeS...  19.1 us
    unnamed x3, local copies, waits for them, and re-layouts  1.61 us

profile of v1, /device:TPU:0, one launch (start us, length us, event | category | flops | bytes accessed | tf_op | source)
XLA Modules:
  0.0 20.8 jit_solution(8257266848934830333)
XLA Ops:
  0.0 0.0 copy-start
  0.0 0.9 %copy-done = bf16[2,2,16,960]{3,2,1,0:T(8,128)(2,1)S(1)} copy-done((bf16[2,2,16,960]{3,2,1,0:T(8,128)(2,1)S(1)}, bf16[2,2,16,960]{3,2,1,0:T(8,128)(2,1)}, u32[]{:S(2)}) %copy-start) | copy-done | bytes 122904
  0.9 19.1 %shard_map.17 = bf16[2,8,32,256]{3,2,1,0:T(8,128)(2,1)S(1)} custom-call(bf16[2,2,16,960]{3,2,1,0:T(8,128)(2,1)S(1)} %copy-done), custom_call_target="tpu_custom_call" | custom-call | flops 1000000000 | bytes 1000000 | tf_op jit(solution)/shard_map/pallas_call | solution.py:254
  20.1 0.7 %copy.3 = bf16[2,8,32,256]{3,2,1,0:T(8,128)(2,1)} copy(bf16[2,8,32,256]{3,2,1,0:T(8,128)(2,1)S(1)} %shard_map.17) | data formatting | bytes 524288
Async XLA Ops:
  0.0 0.9 %copy-start = (bf16[2,2,16,960]{3,2,1,0:T(8,128)(2,1)S(1)}, bf16[2,2,16,960]{3,2,1,0:T(8,128)(2,1)}, u32[]{:S(2)}) copy-start(bf16[2,2,16,960]{3,2,1,0:T(8,128)(2,1)} %x_ref.1) | copy-start | bytes 368644

commit v2 on v1

--- a/solution.py
+++ b/solution.py
@@ -24,16 +24,23 @@
     return jnp.where(hits, 1.0, 0.0).astype(BF16)
 
 
-def kernel(dims, x_ref, out_ref, strips, parts, epochs, lefts, powers, coh, got, *sems):
+def over(value, by):
+    return value >> (by.bit_length() - 1) if by & (by - 1) == 0 else lax.div(value, by)
+
+
+def rest(value, by):
+    return value & (by - 1) if by & (by - 1) == 0 else lax.rem(value, by)
+
+
+def kernel(dims, x_hbm, got, x_ref, strips, parts, epochs, lefts, powers, coh, order, fold, *sems):
     n_epoch, n_space, local, rows, cols, strip = dims
-    send1, recv1, send2, recv2 = sems
+    load, send1, recv1, send2, recv2 = sems
     total = n_epoch * n_space * local
     block = n_space * local
     held = strip + 2 * MARGIN
     width = cols // n_epoch
     lane_pad = strips.shape[-1] // 2
     looks = width // LOOKC
-    all_looks = cols // LOOKC
     lanes = block * looks
     my_i = lax.axis_index("epoch")
     my_j = lax.axis_index("space")
@@ -54,6 +61,8 @@
         if a or b
     ]
 
+    loading = pltpu.make_async_copy(x_hbm, x_ref, load)
+    loading.start()
     barrier = pltpu.get_barrier_semaphore()
     for a, b in steps:
         pl.semaphore_signal(
@@ -65,9 +74,11 @@
 
     cut = (n_space * held * local, local * rows)
     at = iota(cut, 0)
-    strip_of, row_of, own_of = at // (held * local), (at // local) % held, at % local
-    pick_own, pick_row = iota(cut, 1) // rows, iota(cut, 1) % rows
+    strip_of = over(at, held * local)
+    row_of, own_of = rest(over(at, local), held), rest(at, local)
+    pick_own, pick_row = over(iota(cut, 1), rows), rest(iota(cut, 1), rows)
     pick = one_hot((pick_own == own_of) & (pick_row == strip_of * strip + row_of - MARGIN))
+    loading.wait()
     for k in range(2):
         picked = jnp.dot(pick, x_ref[k].reshape(local * rows, cols), preferred_element_type=F32)
         for i in range(n_epoch):
@@ -100,22 +111,24 @@
         copy.start()
         sent.append(copy)
     parts[me] = strips[me]
+    size = total * held
+    to, fro = iota((size, size), 0), iota((size, size), 1)
+    source_row = rest(over(fro, local), held)
+    source_epoch = over(fro, held * local) * local + rest(fro, local)
+    order[...] = one_hot((over(to, total) == source_row) & (rest(to, total) == source_epoch))
+    look = rest(iota((lane_pad, lanes), 1), looks) * LOOKC
+    col = iota((lane_pad, lanes), 0)
+    fold[...] = jnp.where((col >= look) & (col < look + LOOKC), 1.0, 0.0)
     for slot, (a, b) in enumerate(steps):
         from_i, from_j = epoch_source(a), lax.rem(my_j + n_space - b, n_space)
         first_copy(slot, from_i, from_j, from_i * n_space + from_j).wait_recv()
 
-    size = total * held
-    to, fro = iota((size, size), 0), iota((size, size), 1)
-    order = one_hot(
-        (to // total == (fro // local) % held)
-        & (to % total == fro // (held * local) * local + fro % local)
-    )
     arrived = parts[...]
     if (held * local) % 16:
         arrived = arrived.astype(F32).reshape(size, 2 * lane_pad).astype(BF16)
     else:
         arrived = arrived.reshape(size, 2 * lane_pad)
-    by_row = jnp.dot(order, arrived, preferred_element_type=F32)
+    by_row = jnp.dot(order[...], arrived, preferred_element_type=F32)
     epochs[...] = by_row
     re, im = by_row[:, :lane_pad], by_row[:, lane_pad:]
     turned = jnp.concatenate([-im, re], axis=1).astype(BF16)
@@ -130,18 +143,16 @@
         for r in range(strip)
     ]
     summed = jnp.concatenate(summed, axis=0)
-    look = iota((lane_pad, lanes), 1) % looks
-    col = iota((lane_pad, lanes), 0)
-    fold = jnp.where((col >= look * LOOKC) & (col < look * LOOKC + LOOKC), 1.0, 0.0)
-    power = jnp.dot(summed, fold, preferred_element_type=F32, precision=lax.Precision.HIGHEST)
+    power = jnp.dot(summed, fold[...], preferred_element_type=F32, precision=lax.Precision.HIGHEST)
     power = power + 1e-06
     for r in range(strip):
         powers[r] = power[r * total : (r + 1) * total]
 
     window = iota((1, looks, 2 * lane_pad), 1) * LOOKC
-    place = iota((1, looks, 2 * lane_pad), 2) % lane_pad
+    place = iota((1, looks, 2 * lane_pad), 2)
+    place = jnp.where(place < lane_pad, place, place - lane_pad)
     inside = (place >= window) & (place < window + LOOKC)
-    own_lane = iota((block, lanes), 1) // looks == iota((block, lanes), 0)
+    own_lane = over(iota((block, lanes), 1), looks) == iota((block, lanes), 0)
 
     def second_copy(slot, to_i, source):
         return pltpu.make_async_remote_copy(
@@ -192,15 +203,24 @@
         from_i = epoch_source(step)
         second_copy(step, from_i, from_i).wait_recv()
 
+    for copy in sent:
+        copy.wait_send()
+
+
+def spread_kernel(dims, got, out_hbm, out_ref, sem):
+    n_epoch, block, total, strip, all_looks = dims
+    looks = all_looks // n_epoch
+    lanes = block * looks
     if lanes == LANES and (strip * n_epoch) % block == 0 and block & (block - 1) == 0:
-        spot = iota((2 * total, lanes), 1) // looks
+        spot = over(iota((2 * total, lanes), 1), looks)
+        copies = []
         for half in range(strip * n_epoch // block):
             tiles = []
             for t in range(half * block, (half + 1) * block):
                 tiles.append(got[t % n_epoch, t // n_epoch].astype(F32))
             bit = 1
             while bit < block:
-                low = (spot // bit) % 2 == 0
+                low = spot & bit == 0
                 turned_tiles = list(tiles)
                 for t in range(block):
                     if t & bit:
@@ -218,6 +238,15 @@
                     out_ref[k, e, :, half * lanes : (half + 1) * lanes] = value[
                         k * total : (k + 1) * total
                     ]
+            side = pl.ds(half * lanes, lanes)
+            copies.append(
+                pltpu.make_async_copy(
+                    out_ref.at[:, :, :, side], out_hbm.at[:, :, :, side], sem.at[half]
+                )
+            )
+            copies[-1].start()
+        for copy in copies:
+            copy.wait()
     else:
         shape = (lanes, strip * all_looks)
         fro_e, fro_c, goal = iota(shape, 0) // looks, iota(shape, 0) % looks, iota(shape, 1)
@@ -233,9 +262,9 @@
             value = value.astype(BF16)
             for k in range(2):
                 out_ref[k, e] = value[k * total : (k + 1) * total]
-
-    for copy in sent:
-        copy.wait_send()
+        whole = pltpu.make_async_copy(out_ref, out_hbm, sem.at[0])
+        whole.start()
+        whole.wait()
 
 
 def per_device(slc_stack):
@@ -250,20 +279,25 @@
     lanes = block * (width // LOOKC)
     sources = n_epoch * n_space
     dims = (n_epoch, n_space, local, rows, cols, strip)
+    all_looks = cols // LOOKC
     vmem = pl.BlockSpec(memory_space=pltpu.VMEM)
-    return pl.pallas_call(
+    hbm = pl.BlockSpec(memory_space=pl.ANY)
+    got = pl.pallas_call(
         functools.partial(kernel, dims),
-        out_shape=jax.ShapeDtypeStruct((2, block, total, strip * (cols // LOOKC)), BF16),
-        in_specs=[vmem],
+        out_shape=jax.ShapeDtypeStruct((n_epoch, strip, 2 * total, lanes), BF16),
+        in_specs=[hbm],
         out_specs=vmem,
         scratch_shapes=[
+            pltpu.VMEM(slc_stack.shape, BF16),
             pltpu.VMEM((sources, held * local, 2 * lane_pad), BF16),
             pltpu.VMEM((sources, held * local, 2 * lane_pad), BF16),
             pltpu.VMEM((held * total, 2 * lane_pad), F32),
             pltpu.VMEM((held, 2 * total, 2 * lane_pad), BF16),
             pltpu.VMEM((strip, total, lanes), F32),
             pltpu.VMEM((n_epoch, strip, 2 * total, lanes), BF16),
-            pltpu.VMEM((n_epoch, strip, 2 * total, lanes), BF16),
+            pltpu.VMEM((held * total, held * total), BF16),
+            pltpu.VMEM((lane_pad, lanes), F32),
+            pltpu.SemaphoreType.DMA(()),
             pltpu.SemaphoreType.DMA((sources - 1,)),
             pltpu.SemaphoreType.DMA((sources,)),
             pltpu.SemaphoreType.DMA((n_epoch,)),
@@ -274,6 +308,18 @@
         ),
         cost_estimate=pl.CostEstimate(flops=10**9, bytes_accessed=10**6, transcendentals=0),
     )(slc_stack)
+    out = jax.ShapeDtypeStruct((2, block, total, strip * all_looks), BF16)
+    return pl.pallas_call(
+        functools.partial(spread_kernel, (n_epoch, block, total, strip, all_looks)),
+        out_shape=out,
+        in_specs=[vmem],
+        out_specs=hbm,
+        scratch_shapes=[
+            pltpu.VMEM(out.shape, BF16),
+            pltpu.SemaphoreType.DMA((max(1, strip * n_epoch // block),)),
+        ],
+        compiler_params=pltpu.CompilerParams(vmem_limit_bytes=32 * 1024 * 1024),
+    )(got)
 
 
 def solution(mesh):

time: 20.9 us -> 21 us (level)
  Pallas kernels: 19.1 us -> 20 us
  local copies, waits for them, and re-layouts: 1.61 us -> 0.9 us
    pallas_call x0 -> x1, Pallas kernels: none -> 1.09 us  [per_device(): pl.pallas_call(functools.partial(spread_kernel, (n_epoch, block, total, s...]
    unnamed x3 -> x2, local copies, waits for them, and re-layouts: 1.61 us -> 0.9 us
    pallas_call x1, Pallas kernels: 19.1 us -> 18.9 us  [per_device(): pl.pallas_call(functools.partial(kernel, dims), out_shape=jax.ShapeDtypeS...]
where the time goes in v2:
time: 21 us; the launch traced here: 20.9 us
  Pallas kernels  20 us (95%)
  local copies, waits for them, and re-layouts  0.9 us (4%)
    pallas_call x1, Pallas kernels, per_device(): pl.pallas_call(functools.partial(kernel, dims), out_shape=jax.ShapeDtypeS...  18.9 us
    pallas_call x1, Pallas kernels, per_device(): pl.pallas_call(functools.partial(spread_kernel, (n_epoch, block, total, s...  1.09 us
    unnamed x2, local copies, waits for them, and re-layouts  0.9 us

profile of v2, /device:TPU:0, one launch (start us, length us, event | category | flops | bytes accessed | tf_op | source)
XLA Modules:
  0.0 20.9 jit_solution(5073099675219350044)
XLA Ops:
  0.0 0.0 copy-start
  0.0 0.9 %copy-done = bf16[2,2,16,960]{3,2,1,0:T(8,128)(2,1)S(1)} copy-done((bf16[2,2,16,960]{3,2,1,0:T(8,128)(2,1)S(1)}, bf16[2,2,16,960]{3,2,1,0:T(8,128)(2,1)}, u32[]{:S(2)}) %copy-start) | copy-done | bytes 122904
  0.9 18.9 %shard_map.17.got = bf16[4,4,64,128]{3,2,1,0:T(8,128)(2,1)S(1)} custom-call(bf16[2,2,16,960]{3,2,1,0:T(8,128)(2,1)S(1)} %copy-done), custom_call_target="tpu_custom_call" | custom-call | flops 1000000000 | bytes 1000000 | tf_op jit(solution)/shard_map/pallas_call | solution.py:285
  19.8 1.1 %shard_map.18 = bf16[2,8,32,256]{3,2,1,0:T(8,128)(2,1)} custom-call(bf16[4,4,64,128]{3,2,1,0:T(8,128)(2,1)S(1)} %shard_map.17.got), custom_call_target="tpu_custom_call" | custom-call | tf_op jit(solution)/shard_map/pallas_call | solution.py:312
Async XLA Ops:
  0.0 0.9 %copy-start = (bf16[2,2,16,960]{3,2,1,0:T(8,128)(2,1)S(1)}, bf16[2,2,16,960]{3,2,1,0:T(8,128)(2,1)}, u32[]{:S(2)}) copy-start(bf16[2,2,16,960]{3,2,1,0:T(8,128)(2,1)} %x_hbm.1) | copy-start | bytes 368644

commit v3 on v2

--- a/solution.py
+++ b/solution.py
@@ -307,7 +307,7 @@
             collective_id=0, has_side_effects=True, vmem_limit_bytes=48 * 1024 * 1024
         ),
         cost_estimate=pl.CostEstimate(flops=10**9, bytes_accessed=10**6, transcendentals=0),
-    )(slc_stack)
+    )(pltpu.with_memory_space_constraint(slc_stack, pltpu.HBM))
     out = jax.ShapeDtypeStruct((2, block, total, strip * all_looks), BF16)
     return pl.pallas_call(
         functools.partial(spread_kernel, (n_epoch, block, total, strip, all_looks)),

time: 21 us -> 20 us (0.952)
  local copies, waits for them, and re-layouts: 0.9 us -> 0 us
    unnamed x2 -> x0, local copies, waits for them, and re-layouts: 0.9 us -> none
where the time goes in v3:
time: 20 us; the launch traced here: 19.8 us
  Pallas kernels  19.8 us (99%)
    pallas_call x1, Pallas kernels, per_device(): pl.pallas_call(functools.partial(kernel, dims), out_shape=jax.ShapeDtypeS...  18.8 us
    pallas_call x1, Pallas kernels, per_device(): pl.pallas_call(functools.partial(spread_kernel, (n_epoch, block, total, s...  1.09 us

profile of v3, /device:TPU:0, one launch (start us, length us, event | category | flops | bytes accessed | tf_op | source)
XLA Modules:
  0.0 19.8 jit_solution(12876324998490271311)
XLA Ops:
  0.0 18.8 %shard_map.17.got = bf16[4,4,64,128]{3,2,1,0:T(8,128)(2,1)S(1)} custom-call(bf16[2,2,16,960]{3,2,1,0:T(8,128)(2,1)} %x_hbm.1), custom_call_target="tpu_custom_call" | custom-call | flops 1000000000 | bytes 1000000 | tf_op jit(solution)/shard_map/pallas_call | solution.py:285
  18.8 1.1 %shard_map.18 = bf16[2,8,32,256]{3,2,1,0:T(8,128)(2,1)} custom-call(bf16[4,4,64,128]{3,2,1,0:T(8,128)(2,1)S(1)} %shard_map.17.got), custom_call_target="tpu_custom_call" | custom-call | tf_op jit(solution)/shard_map/pallas_call | solution.py:312
